TPU v7x, 32 devices: a whole 2x2x4 slice. The times are simulated.
32 devices in a mesh: node: 8 (over z, core), local: 4 (over y, x).
Axes of the slice: x: 2, y: 2, z: 4, core: 2. Of those that a mesh axis runs over, the one named last changes fastest.
Arguments:
- tokens: bfloat16 [4096, 8192], P(('node', 'local')), may hold values from -6 to 6
- upstream: bfloat16 [4096, 8192], P(('node', 'local')), may hold values from -1.5 to 1.5
- router_probs: float32 [4096, 64], P(('node', 'local')), may hold values from 0.01 to 0.3
- expert_ids: int32 [4096, 2], P(('node', 'local')), may hold values from 0 to 63, as said below
- slot_index: int32 [4096, 2], P(('node', 'local')), may hold values from -1 to 3, as said below
- w_in: bfloat16 [2, 8192, 16384], P(None, 'local', 'node'), may hold values from -0.0625 to 0.0625
- w_out: bfloat16 [2, 16384, 8192], P(None, 'node', 'local'), may hold values from -0.046875 to 0.046875
- router_weight: bfloat16 [8192, 64], replicated, may hold values from -0.125 to 0.125
Outputs:
- token_grads: bfloat16 [4096, 8192], P(('node', 'local'))
- w_in_grad: bfloat16 [2, 8192, 16384], P(None, 'local', 'node')
- w_out_grad: bfloat16 [2, 16384, 8192], P(None, 'node', 'local')
- router_grad: float32 [8192, 64], P(('node', 'local'))
Inputs may be any that keep to these rules, and one draw needn't show every extreme that they name: `expert_ids`: each token names two different experts. `slot_index`: an assignment to an expert under 2 has as slot its rank among its device's 128 tokens' assignments to that expert, in an order drawn at random, and -1 when that rank is 4 or more; every assignment to another expert has -1. In every draw some expert under 2 fills all 4 slots from every device.
All inputs are finite; a program needn't handle non-finite values.
Results may differ from a plain program's by a relative error of at most 0.017.
Values may be sent and summed in bfloat16 or wider, within the bound.
A program may use at most 128 MiB of HBM per device.

v0:
```python
import math

import jax
import jax.numpy as jnp
from jax import lax
from jax.sharding import PartitionSpec as P

CAP = 4


root_two_pi = math.sqrt(2.0 / math.pi)
cubic_coef = 0.044715


def gelu_pair(pre):
    inner = root_two_pi * (pre + cubic_coef * pre * pre * pre)
    tangent = jnp.tanh(inner)
    value = 0.5 * pre * (1.0 + tangent)
    slope = 0.5 * (1.0 + tangent) + 0.5 * pre * (1.0 - tangent * tangent) * root_two_pi * (
        1.0 + 3.0 * cubic_coef * pre * pre
    )
    return (value, slope)


def contract(left, right, left_dim, right_dim):
    return lax.dot_general(
        left, right, (((left_dim,), (right_dim,)), ((), ())), preferred_element_type=jnp.float32
    )


def hidden_step(pre, upw, gate_wide):
    value, slope = gelu_pair(pre)
    act = value.astype(jnp.bfloat16)
    pre_grad = (gate_wide * upw * slope).astype(jnp.bfloat16)
    scores = jnp.sum(act.astype(jnp.float32) * upw, axis=2)
    return (act, pre_grad, scores)


def local(tokens, upstream, router_probs, expert_ids, slot_index, w_in, w_out, router_weight):
    token_count, model_width = tokens.shape
    flight = w_in.shape[0]
    feature_width = w_in.shape[1]
    capacity = CAP
    node_count = lax.axis_size("node")
    local_count = lax.axis_size("local")
    span = local_count * capacity
    is_kept = slot_index >= 0
    target = jnp.where(is_kept, expert_ids * capacity + slot_index, -1)
    slot_iota = jnp.arange(flight * capacity, dtype=jnp.int32)
    slot_hits = slot_iota[:, None, None] == target[None, :, :]
    placing = jnp.any(slot_hits, axis=2).astype(jnp.bfloat16)
    send_in = jnp.dot(placing, tokens, preferred_element_type=jnp.float32).astype(jnp.bfloat16)
    send_up = jnp.dot(placing, upstream, preferred_element_type=jnp.float32).astype(jnp.bfloat16)
    chosen = jnp.take_along_axis(router_probs, expert_ids, axis=1)
    send_gate = jnp.sum(
        jnp.where(slot_hits, chosen[None, :, :], jnp.zeros((), jnp.float32)), axis=(1, 2)
    ).astype(jnp.bfloat16)
    full_in, full_up, full_gate = (
        lax.all_gather(
            send_in.reshape(flight, 1, capacity, model_width), "node", axis=1, tiled=True
        ),
        lax.all_gather(
            send_up.reshape(flight, 1, capacity, model_width), "node", axis=1, tiled=True
        ),
        lax.all_gather(send_gate.reshape(flight, 1, capacity, 1), "node", axis=1, tiled=True),
    )
    in_block = full_in.reshape(flight, node_count, 1, capacity, local_count, feature_width)
    up_block = full_up.reshape(flight, node_count, 1, capacity, local_count, feature_width)
    gate_block = jnp.broadcast_to(
        full_gate.reshape(flight, node_count, 1, capacity, 1, 1),
        (flight, node_count, 1, capacity, local_count, 1),
    )
    got_in, got_up, got_gate = (
        lax.all_to_all(in_block, "local", split_axis=4, concat_axis=2, tiled=True),
        lax.all_to_all(up_block, "local", split_axis=4, concat_axis=2, tiled=True),
        lax.all_to_all(gate_block, "local", split_axis=4, concat_axis=2, tiled=True),
    )
    rows_in = got_in.reshape(flight, -1, feature_width)
    rows_up = got_up.reshape(flight, -1, feature_width)
    gate_wide = got_gate.reshape(flight, -1).astype(jnp.float32)[:, :, None]
    pre_part = jnp.einsum("erd,edf->erf", rows_in, w_in, preferred_element_type=jnp.float32)
    upw_part = jnp.einsum("erd,efd->erf", rows_up, w_out, preferred_element_type=jnp.float32)
    pre, upw = lax.psum((pre_part, upw_part), "local")
    act, pre_grad, score_part = hidden_step(pre, upw, gate_wide)
    out_grad = (gate_wide * rows_up.astype(jnp.float32)).astype(jnp.bfloat16)
    w_out_grad = jnp.einsum(
        "erf,erd->efd", act, out_grad, preferred_element_type=jnp.float32
    ).astype(jnp.bfloat16)
    w_in_grad = jnp.einsum(
        "erd,erf->edf", rows_in, pre_grad, preferred_element_type=jnp.float32
    ).astype(jnp.bfloat16)
    row_terms = jnp.einsum("erf,edf->erd", pre_grad, w_in, preferred_element_type=jnp.float32)
    back_terms, back_scores = (
        lax.psum_scatter(
            row_terms.reshape(flight, node_count, span, feature_width),
            "node",
            scatter_dimension=1,
            tiled=True,
        ),
        lax.psum_scatter(
            score_part.reshape(flight, node_count, span), "node", scatter_dimension=1, tiled=True
        ),
    )
    row_grads = back_terms.astype(jnp.bfloat16).reshape(
        flight, local_count, capacity, 1, feature_width
    )
    home_rows = lax.all_to_all(row_grads, "local", split_axis=1, concat_axis=3, tiled=True).reshape(
        flight * capacity, model_width
    )
    combined = contract(placing, home_rows, 0, 0)
    own_scores = lax.dynamic_slice_in_dim(
        back_scores.reshape(flight, local_count, capacity), lax.axis_index("local"), 1, 1
    ).reshape(-1)
    safe_slot = jnp.where(is_kept, target, 0)
    gate_grad = jnp.where(is_kept, own_scores[safe_slot], jnp.zeros((), jnp.float32))
    expert_count = router_probs.shape[1]
    expert_iota = jnp.arange(expert_count, dtype=jnp.int32)
    matches = expert_ids[:, :, None] == expert_iota[None, None, :]
    prob_grad = jnp.sum(
        jnp.where(matches, gate_grad[:, :, None], jnp.zeros((), jnp.float32)), axis=1
    )
    centred = prob_grad - jnp.sum(router_probs * prob_grad, axis=1, keepdims=True)
    logit_grad = (router_probs * centred).astype(jnp.bfloat16)
    router_grad = lax.psum_scatter(
        contract(tokens, logit_grad, 0, 0), ("node", "local"), scatter_dimension=0, tiled=True
    )
    router_part = contract(logit_grad, router_weight, 1, 1)
    token_grads = (combined + router_part).astype(jnp.bfloat16)
    return (token_grads, w_in_grad, w_out_grad, router_grad)


def solution(mesh):
    in_specs = (
        P(("node", "local"), None),
        P(("node", "local"), None),
        P(("node", "local"), None),
        P(("node", "local"), None),
        P(("node", "local"), None),
        P(None, "local", "node"),
        P(None, "node", "local"),
        P(),
    )
    out_specs = (
        P(("node", "local"), None),
        P(None, "local", "node"),
        P(None, "node", "local"),
        P(("node", "local"), None),
    )
    return jax.shard_map(local, mesh=mesh, in_specs=in_specs, out_specs=out_specs, check_vma=False)
```

profile of v0, /device:TPU:0, one launch (start us, length us, event | category | flops | bytes accessed | tf_op | source)
XLA Modules:
  0.0 415.7 jit_solution(6177130709805882613)
XLA Ops:
  12.7 22.3 %all-gather.5.cloned.1.call-done = bf16[2,8,4,8192]{3,2,0,1:T(4,128)(2,1)} async-done(((bf16[2,1,4,8192]{3,2,0,1:T(4,128)(2,1)}), bf16[2,8,4,8192]{3,2,0,1:T(4,128)(2,1)}) %all-gather.5.cloned.1.call-update) | async-done | bytes 1048592 | tf_op jit(solution)/shard_map/all_gather | solution.py:59
  38.7 3.6 all-to-all-start.2
  42.3 16.8 %all-gather.3.cloned.1.call-done = bf16[2,8,4,8192]{3,2,0,1:T(4,128)(2,1)} async-done(((bf16[2,1,4,8192]{3,2,0,1:T(4,128)(2,1)}), bf16[2,8,4,8192]{3,2,0,1:T(4,128)(2,1)}) %all-gather.3.cloned.1.call-update) | async-done | bytes 1048592 | tf_op jit(solution)/shard_map/all_gather | solution.py:62
  59.1 2.6 reshape.93
  61.7 3.0 copy.198
  64.7 4.2 %all-to-all-start.1 = ((bf16[2,8,1,4,4,2048]{5,3,1,0,2,4:T(4,128)(2,1)}), bf16[2,8,1,4,4,2048]{5,3,1,0,2,4:T(4,128)(2,1)}, u32[]{:S(2)}, u32[]{:S(2)}) async-start(bf16[2,8,1,4,4,2048]{5,3,1,0,2,4:T(4,128)(2,1)} %copy.198), calls=%async_computation.1 | async-start | bytes 2097152 | tf_op jit(solution)/shard_map/all_to_all | solution.py:75
  71.9 11.4 %all-to-all-done.1 = bf16[2,8,1,4,4,2048]{5,3,1,0,2,4:T(4,128)(2,1)} async-done(((bf16[2,8,1,4,4,2048]{5,3,1,0,2,4:T(4,128)(2,1)}), bf16[2,8,1,4,4,2048]{5,3,1,0,2,4:T(4,128)(2,1)}, u32[]{:S(2)}, u32[]{:S(2)}) %all-to-all-start.1) | async-done | bytes 1048608 | tf_op jit(solution)/shard_map/all_to_all | solution.py:75
  83.3 2.8 copy.199
  86.1 2.1 reshape.94
  88.2 13.1 %fusion.12 = f32[2,128,2048]{2,1,0:T(8,128)} fusion(bf16[2,128,2048]{2,1,0:T(8,128)(2,1)} %reshape.94, bf16[2,2048,2048]{2,1,0:T(8,128)(2,1)} %param.14), kind=kOutput, calls=%fused_computation.46 | convolution fusion | flops 2147483648 | bytes 19922944 | tf_op jit(solution)/shard_map/erd,efd->erf/dot_general | solution.py:82
  101.3 9.4 %fusion.13 = f32[2,128,2048]{2,1,0:T(8,128)} fusion(bf16[2,128,2048]{2,1,0:T(8,128)(2,1)S(1)} %reshape.97, bf16[2,2048,2048]{2,1,0:T(8,128)(2,1)} %param.13), kind=kOutput, calls=%fused_computation.47 | convolution fusion | flops 2147483648 | bytes 19922944 | tf_op jit(solution)/shard_map/erd,edf->erf/dot_general | solution.py:81
  114.1 10.3 %all_gather.9 = bf16[2,8,4,1]{2,0,3,1:T(2,128)(2,1)S(1)} all-gather(bf16[2,1,4,1]{2,0,3,1:T(2,128)(2,1)S(1)} %convert_element_type.67), channel_id=1, replica_groups=mesh['node'=8,'local'=4] {'node'}, dimensions={1}, use_global_device_ids=true | all-gather | bytes 144 | tf_op jit(solution)/shard_map/all_gather | solution.py:65
  124.5 7.3 %all_to_all.54 = bf16[2,8,1,4,4,1]{1,3,5,2,0,4:T(4,128)(2,1)S(1)} all-to-all(bf16[2,8,1,4,4,1]{1,3,5,2,0,4:T(4,128)(2,1)S(1)} %broadcast_in_dim.60), channel_id=1, replica_groups=mesh['node'=8,'local'=4] {'local'}, dimensions={4} | all-to-all | bytes 1024 | tf_op jit(solution)/shard_map/all_to_all | solution.py:76
  132.1 81.9 %all-reduce.4.cloned.1.call-done = (f32[2,128,2048]{2,1,0:T(8,128)}, f32[2,128,2048]{2,1,0:T(8,128)}) async-done(((f32[2,128,2048]{2,1,0:T(8,128)}, f32[2,128,2048]{2,1,0:T(8,128)}), (f32[2,128,2048]{2,1,0:T(8,128)}, f32[2,128,2048]{2,1,0:T(8,128)})) %all-reduce.4.cloned.1.call-update) | async-done | bytes 4194320 | tf_op jit(solution)/shard_map/psum | solution.py:83
  214.0 4.3 %multiply_reduce_fusion = (f32[2,128]{1,0:T(2,128)S(1)}, bf16[2,128,2048]{2,1,0:T(8,128)(2,1)}) fusion(f32[2,128,2048]{2,1,0:T(8,128)} %get-tuple-element.5, f32[2,128,2048]{2,1,0:T(8,128)} %get-tuple-element.4, f32[2,128]{1,0:T(2,128)S(1)} %reshape.104), kind=kLoop, calls=%fused_computation.18 | loop fusion | flops 13106944 | bytes 5244928 | tf_op jit(solution)/shard_map/reduce_sum | solution.py:35
  218.3 13.0 %fusion.14 = f32[2,128,2048]{2,1,0:T(8,128)} fusion(bf16[2,128,2048]{2,1,0:T(8,128)(2,1)} %get-tuple-element.7, bf16[2,2048,2048]{2,1,0:T(8,128)(2,1)} %param.13), kind=kOutput, calls=%fused_computation.48 | convolution fusion | flops 2147483648 | bytes 19922944 | tf_op jit(solution)/shard_map/erf,edf->erd/dot_general | solution.py:92
  231.3 3.1 copy.202
  235.8 17.0 %all-reduce = f32[2,8,16]{2,0,1:T(2,128)S(1)} all-reduce(f32[2,8,16]{2,0,1:T(2,128)S(1)} %copy.206), channel_id=3, replica_groups=mesh['node'=8,'local'=4] {'node'}, use_global_device_ids=true, to_apply=%region_6.7.clone | all-reduce | flops 256 | bytes 2048
  254.3 4.9 %fusion.10 = f32[128,2]{0,1:T(2,128)S(1)} fusion(f32[]{:T(128)} %bitcast.13, f32[]{:T(128)} %bitcast.14, f32[]{:T(128)} %bitcast.15, f32[]{:T(128)} %bitcast.16, f32[]{:T(128)} %bitcast.17, f32[]{:T(128)} %bitcast.18, f32[]{:T(128)} %bitcast.19, f32[]{:T(128)} %bitcast.20, s32[128,2]{0,1:T(2,128)S(1)} %copy-done.4, s32[128,2]{0,1:T(2,128)S(1)} %copy-done.3), kind=kLoop, calls=%fused_computation.39 | loop fusion | flops 5888 | bytes 3104 | tf_op jit(solution)/shard_map/jit(_where)/select_n | solution.py:115
  261.0 12.6 %convolution_convert_fusion = bf16[2,2048,2048]{2,1,0:T(8,128)(2,1)} fusion(bf16[2,128,2048]{2,1,0:T(8,128)(2,1)} %reshape.94, f32[2,128]{1,0:T(2,128)S(1)} %reshape.104, f32[2,128,2048]{2,1,0:T(8,128)} %get-tuple-element.4), kind=kOutput, calls=%fused_computation.1 | convolution fusion | flops 2162163712 | bytes 19923968 | tf_op jit(solution)/shard_map/erf,erd->efd/dot_general | solution.py:86
  275.4 3.5 all-to-all-start.3
  279.0 9.8 %convolution_convert_fusion.1 = bf16[2,2048,2048]{2,1,0:T(8,128)(2,1)} fusion(bf16[2,128,2048]{2,1,0:T(8,128)(2,1)S(1)} %reshape.97, bf16[2,128,2048]{2,1,0:T(8,128)(2,1)} %get-tuple-element.7), kind=kOutput, calls=%fused_computation.2 | convolution fusion | flops 2155872256 | bytes 18874368 | tf_op jit(solution)/shard_map/erd,erf->edf/dot_general | solution.py:89
  290.2 2.1 fusion
  292.3 116.9 %reduce-scatter.5.cloned.1.call-done = f32[256,64]{0,1:T(8,128)} async-done(((f32[8192,64]{0,1:T(8,128)}), f32[256,64]{0,1:T(8,128)}) %reduce-scatter.5.cloned.1.call-update) | async-done | bytes 65552 | tf_op jit(solution)/shard_map/reduce_scatter | solution.py:124
  (66 shorter events, 23.5 us)
Async XLA Ops:
  7.2 1.6 copy-start
  7.2 27.8 %all-gather.5.cloned.1.call-start = ((), (), s32[]{:S(2)}) async-start(), calls=%async_computation.7 | async-start | bytes 1179648 | tf_op jit(solution)/shard_map/all_gather | solution.py:59
  9.9 49.2 %all-gather.3.cloned.1.call-start = ((), (), s32[]{:S(2)}) async-start(), calls=%async_computation.6 | async-start | bytes 1179648 | tf_op jit(solution)/shard_map/all_gather | solution.py:62
  38.7 26.1 %all-to-all-start.2 = ((bf16[2,8,1,4,4,2048]{5,3,1,0,2,4:T(4,128)(2,1)}), bf16[2,8,1,4,4,2048]{5,3,1,0,2,4:T(4,128)(2,1)S(1)}, u32[]{:S(2)}, u32[]{:S(2)}) async-start(bf16[2,8,1,4,4,2048]{5,3,1,0,2,4:T(4,128)(2,1)} %copy.200), calls=%async_computation.2 | async-start | bytes 2097152 | tf_op jit(solution)/shard_map/all_to_all | solution.py:74
  64.7 18.6 %all-to-all-start.1 = ((bf16[2,8,1,4,4,2048]{5,3,1,0,2,4:T(4,128)(2,1)}), bf16[2,8,1,4,4,2048]{5,3,1,0,2,4:T(4,128)(2,1)}, u32[]{:S(2)}, u32[]{:S(2)}) async-start(bf16[2,8,1,4,4,2048]{5,3,1,0,2,4:T(4,128)(2,1)} %copy.198), calls=%async_computation.1 | async-start | bytes 2097152 | tf_op jit(solution)/shard_map/all_to_all | solution.py:75
  69.0 145.0 %all-reduce.4.cloned.1.call-start = ((), (), s32[]{:S(2)}) async-start(), calls=%async_computation.10 | async-start | bytes 8388608 | tf_op jit(solution)/shard_map/psum | solution.py:83
  110.7 0.7 copy-start.3
  110.7 0.9 copy-start.1
  110.8 162.9 %reduce-scatter.3.cloned.1.call-start = ((), (), s32[]{:S(2)}) async-start(), calls=%async_computation.8 | async-start | bytes 2359296 | tf_op jit(solution)/shard_map/reduce_scatter | solution.py:94
  234.5 0.7 copy-start.5
  234.5 19.8 %copy-start.4 = (s32[128,2]{0,1:T(2,128)S(1)}, s32[128,2]{0,1:T(2,128)}, u32[]{:S(2)}) copy-start(s32[128,2]{0,1:T(2,128)} %param.12) | copy-start | bytes 3076
  234.5 174.7 %reduce-scatter.5.cloned.1.call-start = ((), (), s32[]{:S(2)}) async-start(), calls=%async_computation.9 | async-start | bytes 2162688 | tf_op jit(solution)/shard_map/reduce_scatter | solution.py:124
  275.4 13.3 %all-to-all-start.3 = ((bf16[2,4,4,1,2048]{4,0,2,3,1:T(2,128)(2,1)}), bf16[2,4,4,1,2048]{4,0,2,3,1:T(2,128)(2,1)S(1)}, u32[]{:S(2)}, u32[]{:S(2)}) async-start(bf16[2,4,4,1,2048]{4,0,2,3,1:T(2,128)(2,1)} %bitcast.10), calls=%async_computation.4 | async-start | bytes 262144 | tf_op jit(solution)/shard_map/all_to_all | solution.py:107
  288.9 1.2 copy-start.2
Sparse Core Ops, SparseCore 0:
  10.2 24.7 all-gather.4
  37.2 21.8 all-gather.2
  110.9 103.0 all-reduce.3
  234.6 35.9 reduce-scatter.2
  273.4 135.7 reduce-scatter.4
where the time goes:
time: 417 us; the launch traced here: 416 us
  waiting for transfers between devices  249 us (60%)
  matrix products  64.9 us (16%)
  blocking collectives  34.6 us (8%)
  local copies, waits for them, and re-layouts  30 us (7%)
  between operations  13.9 us (3%)
  starting transfers between devices  11.6 us (3%)
  other arithmetic  11.2 us (3%)
    reduce_scatter x1, waiting for transfers between devices, local(): lax.psum_scatter(contract(tokens, logit_grad, 0, 0), ('node', 'local'), s...  117 us
    psum x1, waiting for transfers between devices, local(): pre, upw = lax.psum((pre_part, upw_part), 'local')  81.9 us
    all_gather x1, waiting for transfers between devices, local(): lax.all_gather(send_in.reshape(flight, 1, capacity, model_width), 'node',...  22.3 us
    unnamed x1, blocking collectives  17 us
    all_gather x1, waiting for transfers between devices, local(): lax.all_gather(send_up.reshape(flight, 1, capacity, model_width), 'node',...  16.8 us
    dot_general x1, matrix products, local(): jnp.einsum('erd,efd->erf', rows_up, w_out, preferred_element_type=jnp.flo...  13.1 us
    dot_general x1, matrix products, local(): jnp.einsum('erf,edf->erd', pre_grad, w_in, preferred_element_type=jnp.flo...  13 us
    dot_general x1, matrix products, local(): jnp.einsum('erf,erd->efd', act, out_grad, preferred_element_type=jnp.floa...  12.6 us
  transfers between devices with their start and end apart: 8, of which 5 were waited for; matrix products, arithmetic and copies ran while one was open for 13% of the time, Pallas kernels for 0%

commit v1 on v0

v1 whole, which is shorter than its diff:
```python
import math

import jax
import jax.numpy as jnp
from jax import lax
from jax.experimental import pallas as pl
from jax.experimental.pallas import tpu as pltpu
from jax.sharding import PartitionSpec as P

CAP = 4
PAD = 128
MESH = pl.DeviceIdType.MESH
VMEM_BYTES = 60 * 1024 * 1024


root_two_pi = math.sqrt(2.0 / math.pi)
cubic_coef = 0.044715


def gelu_pair(pre):
    inner = root_two_pi * (pre + cubic_coef * pre * pre * pre)
    tangent = jnp.tanh(inner)
    value = 0.5 * pre * (1.0 + tangent)
    slope = 0.5 * (1.0 + tangent) + 0.5 * pre * (1.0 - tangent * tangent) * root_two_pi * (
        1.0 + 3.0 * cubic_coef * pre * pre
    )
    return (value, slope)


def contract(left, right, left_dim, right_dim):
    return lax.dot_general(
        left, right, (((left_dim,), (right_dim,)), ((), ())), preferred_element_type=jnp.float32
    )


def one_hot_rows(out_rows, in_rows, source):
    at = lax.broadcasted_iota(jnp.int32, (out_rows, in_rows), 0)
    column = lax.broadcasted_iota(jnp.int32, (out_rows, in_rows), 1)
    return (source(at) == column).astype(jnp.bfloat16)


def gate_column(blocks, expert):
    flat = blocks.reshape(-1, PAD).astype(jnp.float32)
    lane = lax.broadcasted_iota(jnp.int32, flat.shape, 1)
    return jnp.sum(jnp.where(lane == expert, flat, 0.0), axis=1, keepdims=True)


def exchange(dims, send, w_in, w_out, rows_out, hidden_out, scores_out, home_out,
             w_in_v, w_out_v, first, rows_v, part_s, part_r, own, hidden_v, terms, terms_r,
             core_sum, node_r, grads, home_s, home_r, score_1, score_2, score_3,
             w_sem, out_sem, a_s, a_r, z_s, z_r, c_s, c_r, p_s, p_r, g_s, g_r, t_s, t_r,
             n_s, n_r, h_s, h_r, s1_s, s1_r, s2_s, s2_r, s3_s, s3_r):
    nodes, locals_, flight, width, hidden = dims
    chips = nodes // 2
    span = locals_ * CAP
    rows = nodes * span
    piece = hidden // locals_
    node = lax.axis_index("node")
    loc = lax.axis_index("local")
    core = lax.rem(node, 2)
    chip = node // 2

    def local_peer(d):
        return (node, lax.rem(loc + d, locals_))

    def chip_peer(d):
        return (lax.rem(chip + d, chips) * 2 + core, loc)

    sibling = (chip * 2 + 1 - core, loc)
    peers = [local_peer(d) for d in range(1, locals_)]
    peers += [chip_peer(d) for d in range(1, chips)] + [sibling]

    def remote(src, dst, send_sem, recv_sem, peer):
        return pltpu.make_async_remote_copy(
            src_ref=src, dst_ref=dst, send_sem=send_sem, recv_sem=recv_sem,
            device_id=peer, device_id_type=MESH,
        )

    loads = []
    for e in range(flight):
        loads.append(pltpu.make_async_copy(w_in.at[e], w_in_v.at[e], w_sem.at[2 * e]))
        loads.append(pltpu.make_async_copy(w_out.at[e], w_out_v.at[e], w_sem.at[2 * e + 1]))
    for load in loads:
        load.start()

    barrier = pltpu.get_barrier_semaphore()
    for peer in peers:
        pl.semaphore_signal(barrier, inc=1, device_id=peer, device_id_type=MESH)
    pl.semaphore_wait(barrier, len(peers))

    sent = []

    def launch(copies):
        for copy in copies:
            copy.start()
        sent.extend(copies)
        return copies

    def arrive(copies):
        for copy in copies:
            copy.wait_recv()

    moved = launch([
        remote(send.at[lax.rem(loc + d, locals_)], first.at[loc], a_s.at[d], a_r.at[d], local_peer(d))
        for d in range(1, locals_)
    ])
    first[loc] = send[loc]
    arrive(moved)
    kinds = 2 * flight
    block = kinds * CAP

    def gather_source(i):
        k, rest = i // span, lax.rem(i, span)
        return (rest // CAP) * block + k * CAP + lax.rem(rest, CAP)

    order = one_hot_rows(kinds * span, locals_ * block, gather_source)
    ordered = contract(order, first[...].reshape(locals_ * block, width + PAD), 1, 0)
    ordered = ordered.astype(jnp.bfloat16)
    for e in range(flight):
        rows_v[e, node] = ordered[e * 2 * span:(e + 1) * 2 * span]

    def to_chips(e):
        copies = launch([
            remote(rows_v.at[e, node], rows_v.at[e, node], z_s.at[e, d], z_r.at[e, d], chip_peer(d))
            for d in range(1, chips)
        ])
        return copies, launch([
            remote(rows_v.at[e, node], rows_v.at[e, node], c_s.at[e, 0], c_r.at[e, 0], sibling)
        ])

    def finish_rows(e, copies, over):
        for d in range(1, chips):
            copies[d - 1].wait_recv()
            at = lax.rem(chip + chips - d, chips) * 2 + core
            over = over + launch([
                remote(rows_v.at[e, at], rows_v.at[e, at], c_s.at[e, d], c_r.at[e, d], sibling)
            ])
        return over

    def project(e):
        loads[2 * e].wait()
        loads[2 * e + 1].wait()
        left = rows_v[e, :, 0:span, 0:width].reshape(rows, width)
        up = rows_v[e, :, span:2 * span, 0:width].reshape(rows, width)
        copies = []
        tile = min(piece, 256)
        for d in list(range(1, locals_)) + [0]:
            base = lax.rem(loc + d, locals_) * piece

            def column(j, carry):
                at = pl.ds(pl.multiple_of(base + j * tile, tile), tile)
                to = pl.ds(pl.multiple_of(j * tile, tile), tile)
                pre = contract(left, w_in_v[e, :, at], 1, 0)
                upw = contract(up, w_out_v[e, at, :], 1, 1)
                if d == 0:
                    own[0, :, to] = pre
                    own[1, :, to] = upw
                else:
                    part_s[e, d - 1, 0, :, to] = pre.astype(jnp.bfloat16)
                    part_s[e, d - 1, 1, :, to] = upw.astype(jnp.bfloat16)
                return carry

            lax.fori_loop(0, piece // tile, column, 0)
            if d > 0:
                copies += launch([
                    remote(part_s.at[e, d - 1], part_r.at[e, d - 1], p_s.at[e, d], p_r.at[e, d],
                           local_peer(d))
                ])
        return copies

    def hidden_step(e, copies):
        arrive(copies)
        gate = gate_column(rows_v[e, :, 0:span, width:width + PAD], e)
        pre, upw = own[0], own[1]
        for d in range(locals_ - 1):
            pre = pre + part_r[e, d, 0].astype(jnp.float32)
            upw = upw + part_r[e, d, 1].astype(jnp.float32)
        value, slope = gelu_pair(pre)
        act = value.astype(jnp.bfloat16)
        here = pl.ds(pl.multiple_of(loc * piece, piece), piece)
        hidden_v[e, 0, :, here] = act
        hidden_v[e, 1, :, here] = (gate * upw * slope).astype(jnp.bfloat16)
        score_1[loc, 8 * e:8 * e + 8] = lax.dot_general(
            jnp.ones((8, piece), jnp.float32), act.astype(jnp.float32) * upw,
            (((1,), (1,)), ((), ())), precision=lax.Precision.HIGHEST,
            preferred_element_type=jnp.float32,
        )
        mine = hidden_v.at[e, :, :, here]
        return launch([
            remote(mine, mine, g_s.at[e, d], g_r.at[e, d], local_peer(d)) for d in range(1, locals_)
        ])

    def row_terms(e, copies):
        arrive(copies)
        tile = min(width, 512)

        def column(j, carry):
            at = pl.ds(pl.multiple_of(j * tile, tile), tile)
            made = contract(hidden_v[e, 1], w_in_v[e, at, :], 1, 1).astype(jnp.bfloat16)
            terms[e, :, :, :, at] = made.reshape(chips, 2, span, tile)
            return carry

        lax.fori_loop(0, width // tile, column, 0)
        return launch([
            remote(terms.at[e, :, 1 - core], terms_r.at[e], t_s.at[e], t_r.at[e], sibling)
        ])

    def reduce_nodes(e, copies):
        arrive(copies)
        core_sum[e] = (
            terms[e, :, core].astype(jnp.float32) + terms_r[e].astype(jnp.float32)
        ).astype(jnp.bfloat16)
        return launch([
            remote(core_sum.at[e, lax.rem(chip + d, chips)], node_r.at[e, d - 1], n_s.at[e, d],
                   n_r.at[e, d], chip_peer(d))
            for d in range(1, chips)
        ])

    def finish_grads(e, copies):
        arrive(copies)
        total = core_sum[e, chip].astype(jnp.float32)
        for d in range(chips - 1):
            total = total + node_r[e, d].astype(jnp.float32)
        grads[e] = total.astype(jnp.bfloat16)

    z_0, over_0 = to_chips(0)
    over_0 = finish_rows(0, z_0, over_0)
    z_1, over_1 = to_chips(1)
    arrive(over_0)
    parts_0 = project(0)
    over_1 = finish_rows(1, z_1, over_1)
    hidden_0 = hidden_step(0, parts_0)
    arrive(over_1)
    rows_copy = pltpu.make_async_copy(rows_v, rows_out, out_sem.at[0])
    rows_copy.start()
    parts_1 = project(1)
    terms_0 = row_terms(0, hidden_0)
    hidden_1 = hidden_step(1, parts_1)

    near = launch([
        remote(score_1.at[loc], score_1.at[loc], s1_s.at[d], s1_r.at[d], local_peer(d))
        for d in range(1, locals_)
    ])
    nodes_0 = reduce_nodes(0, terms_0)
    arrive(near)
    score_2[chip] = jnp.sum(score_1[...], axis=0)
    along = launch([
        remote(score_2.at[chip], score_2.at[chip], s2_s.at[d], s2_r.at[d], chip_peer(d))
        for d in range(1, chips)
    ])
    terms_1 = row_terms(1, hidden_1)
    hidden_copy = pltpu.make_async_copy(hidden_v, hidden_out, out_sem.at[1])
    hidden_copy.start()
    arrive(along)
    score_3[core] = jnp.sum(score_2[...], axis=0)
    across = launch([
        remote(score_3.at[core], score_3.at[core], s3_s.at[0], s3_r.at[0], sibling)
    ])
    nodes_1 = reduce_nodes(1, terms_1)
    finish_grads(0, nodes_0)
    arrive(across)
    scores_out[...] = score_3[0] + score_3[1]
    finish_grads(1, nodes_1)

    def home_source(i):
        at, rest = i // (flight * CAP), lax.rem(i, flight * CAP)
        return (rest // CAP) * span + at * CAP + lax.rem(rest, CAP)

    pick = one_hot_rows(locals_ * flight * CAP, flight * span, home_source)
    picked = contract(pick, grads[...].reshape(flight * span, width), 1, 0)
    home_s[...] = picked.reshape(locals_, flight * CAP, width)
    home = launch([
        remote(home_s.at[lax.rem(loc + d, locals_)], home_r.at[loc], h_s.at[d], h_r.at[d],
               local_peer(d))
        for d in range(1, locals_)
    ])
    home_r[loc] = home_s[loc]
    arrive(home)
    home_out[...] = home_r[...]
    for copy in sent:
        copy.wait_send()
    rows_copy.wait()
    hidden_copy.wait()


def run_exchange(send, w_in, w_out, nodes, locals_):
    flight, width, hidden = w_in.shape
    chips = nodes // 2
    span = locals_ * CAP
    rows = nodes * span
    piece = hidden // locals_
    wide = width + PAD
    block = send.shape[1]
    half, full = jnp.bfloat16, jnp.float32
    dma = pltpu.SemaphoreType.DMA
    vmem = pl.BlockSpec(memory_space=pltpu.VMEM)
    hbm = pl.BlockSpec(memory_space=pl.ANY)

    def kernel(*refs):
        exchange((nodes, locals_, flight, width, hidden), *refs)

    return pl.pallas_call(
        kernel,
        out_shape=(
            jax.ShapeDtypeStruct((flight, nodes, 2 * span, wide), half),
            jax.ShapeDtypeStruct((flight, 2, rows, hidden), half),
            jax.ShapeDtypeStruct((flight * 8, rows), full),
            jax.ShapeDtypeStruct((locals_, flight * CAP, width), full),
        ),
        in_specs=[vmem, hbm, hbm],
        out_specs=(hbm, hbm, vmem, vmem),
        scratch_shapes=[
            pltpu.VMEM((flight, width, hidden), half),
            pltpu.VMEM((flight, hidden, width), half),
            pltpu.VMEM((locals_, block, wide), half),
            pltpu.VMEM((flight, nodes, 2 * span, wide), half),
            pltpu.VMEM((flight, locals_ - 1, 2, rows, piece), half),
            pltpu.VMEM((flight, locals_ - 1, 2, rows, piece), half),
            pltpu.VMEM((2, rows, piece), full),
            pltpu.VMEM((flight, 2, rows, hidden), half),
            pltpu.VMEM((flight, chips, 2, span, width), half),
            pltpu.VMEM((flight, chips, span, width), half),
            pltpu.VMEM((flight, chips, span, width), half),
            pltpu.VMEM((flight, chips - 1, span, width), half),
            pltpu.VMEM((flight, span, width), half),
            pltpu.VMEM((locals_, flight * CAP, width), full),
            pltpu.VMEM((locals_, flight * CAP, width), full),
            pltpu.VMEM((locals_, flight * 8, rows), full),
            pltpu.VMEM((chips, flight * 8, rows), full),
            pltpu.VMEM((2, flight * 8, rows), full),
            dma((2 * flight,)), dma((2,)),
            dma((locals_,)), dma((locals_,)),
            dma((flight, chips)), dma((flight, chips)),
            dma((flight, chips)), dma((flight, chips)),
            dma((flight, locals_)), dma((flight, locals_)),
            dma((flight, locals_)), dma((flight, locals_)),
            dma((flight,)), dma((flight,)),
            dma((flight, chips)), dma((flight, chips)),
            dma((locals_,)), dma((locals_,)),
            dma((locals_,)), dma((locals_,)),
            dma((chips,)), dma((chips,)),
            dma((1,)), dma((1,)),
        ],
        compiler_params=pltpu.CompilerParams(
            collective_id=0, has_side_effects=True, vmem_limit_bytes=VMEM_BYTES
        ),
        cost_estimate=pl.CostEstimate(
            flops=6 * flight * rows * width * hidden,
            bytes_accessed=4 * flight * width * hidden,
            transcendentals=flight * rows * piece,
        ),
        name="exchange",
    )(send, w_in, w_out)


def weight_grads(rows_all, hidden_all, width):
    flight, nodes, double, wide = rows_all.shape
    span = double // 2
    rows, hidden = hidden_all.shape[2:]
    steps = 8
    high, low = hidden // steps, width // steps

    def kernel(rows_ref, act_ref, grad_ref, left_ref, out_ref, in_ref, out_grad):
        e, step = pl.program_id(0), pl.program_id(1)

        @pl.when(step == 0)
        def _():
            gate = gate_column(rows_ref[0, :, 0:span, width:wide], e)
            up = rows_ref[0, :, span:double, 0:width].reshape(rows, width)
            out_grad[...] = (gate * up.astype(jnp.float32)).astype(jnp.bfloat16)

        out_ref[0] = contract(act_ref[0, 0], out_grad[...], 0, 0).astype(jnp.bfloat16)
        left = left_ref[0, :, 0:span].reshape(rows, low)
        in_ref[0] = contract(left, grad_ref[0, 0], 0, 0).astype(jnp.bfloat16)

    return pl.pallas_call(
        kernel,
        grid=(flight, steps),
        in_specs=[
            pl.BlockSpec((1, nodes, double, wide), lambda e, s: (e, 0, 0, 0)),
            pl.BlockSpec((1, 1, rows, high), lambda e, s: (e, 0, 0, s)),
            pl.BlockSpec((1, 1, rows, hidden), lambda e, s: (e, 1, 0, 0)),
            pl.BlockSpec((1, nodes, double, low), lambda e, s: (e, 0, 0, s)),
        ],
        out_specs=(
            pl.BlockSpec((1, high, width), lambda e, s: (e, s, 0)),
            pl.BlockSpec((1, low, hidden), lambda e, s: (e, s, 0)),
        ),
        out_shape=(
            jax.ShapeDtypeStruct((flight, hidden, width), jnp.bfloat16),
            jax.ShapeDtypeStruct((flight, width, hidden), jnp.bfloat16),
        ),
        scratch_shapes=[pltpu.VMEM((rows, width), jnp.bfloat16)],
        compiler_params=pltpu.CompilerParams(vmem_limit_bytes=40 * 1024 * 1024),
        cost_estimate=pl.CostEstimate(
            flops=4 * flight * rows * width * hidden,
            bytes_accessed=4 * flight * width * hidden,
            transcendentals=0,
        ),
        name="weight_grads",
    )(rows_all, hidden_all, hidden_all, rows_all)


def local(tokens, upstream, router_probs, expert_ids, slot_index, w_in, w_out, router_weight):
    model_width = tokens.shape[1]
    flight, width = w_in.shape[:2]
    experts = router_probs.shape[1]
    nodes = lax.axis_size("node")
    locals_ = lax.axis_size("local")
    node = lax.axis_index("node")
    span = locals_ * CAP
    rows = nodes * span
    is_kept = slot_index >= 0
    target = jnp.where(is_kept, expert_ids * CAP + slot_index, -1)
    slot_iota = jnp.arange(flight * CAP, dtype=jnp.int32)
    slot_hits = slot_iota[:, None, None] == target[None, :, :]
    placing = jnp.any(slot_hits, axis=2).astype(jnp.bfloat16)
    high = router_probs.astype(jnp.bfloat16)
    low = (router_probs - high.astype(jnp.float32)).astype(jnp.bfloat16)
    room = jnp.zeros((high.shape[0], PAD // 2 - experts), jnp.bfloat16)
    probs = jnp.concatenate([high, room, low, room], axis=1)

    def place(array):
        return jnp.dot(placing, array, preferred_element_type=jnp.float32).astype(jnp.bfloat16)

    feats = jnp.stack(
        [place(tokens).reshape(flight, CAP, locals_, width),
         place(upstream).reshape(flight, CAP, locals_, width)], axis=1
    ).reshape(flight * 2 * CAP, locals_, width)
    tail = jnp.broadcast_to(
        place(probs).reshape(flight, 1, CAP, 1, PAD), (flight, 2, CAP, locals_, PAD)
    ).reshape(flight * 2 * CAP, locals_, PAD)
    send = jnp.swapaxes(jnp.concatenate([feats, tail], axis=2), 0, 1)

    rows_all, hidden_all, scores, home = run_exchange(send, w_in, w_out, nodes, locals_)
    w_out_grad, w_in_grad = weight_grads(rows_all, hidden_all, width)

    both = rows_all[:, :, 0:span, width:].reshape(flight, rows, 2, PAD // 2)[:, :, :, :experts]
    probs_rows = both[:, :, 0].astype(jnp.float32) + both[:, :, 1].astype(jnp.float32)
    own_prob = jnp.stack([probs_rows[e, :, e] for e in range(flight)])
    score = scores.reshape(flight, 8, rows)[:, 0, :, None]
    hot = (jnp.arange(experts)[None, :] == jnp.arange(flight)[:, None]).astype(jnp.float32)
    logit_rows = probs_rows * ((hot[:, None, :] - own_prob[:, :, None]) * score)
    logit_rows = logit_rows.astype(jnp.bfloat16)

    block = width // nodes
    picked = lax.dynamic_slice_in_dim(rows_all[:, :, 0:span], node * block, block, 3)
    part = contract(
        picked.reshape(flight * rows, block), logit_rows.reshape(flight * rows, experts), 0, 0
    )
    pairs = [
        (n * locals_ + l, nodes * l + n) for n in range(nodes) for l in range(locals_)
    ]
    router_grad = lax.ppermute(part, ("node", "local"), pairs)

    me = node * locals_ + lax.axis_index("local")
    home_logits = lax.dynamic_slice_in_dim(
        logit_rows.reshape(flight, nodes * locals_, CAP, experts), me, 1, 1
    )
    router_part = contract(home_logits.reshape(flight * CAP, experts), router_weight, 1, 1)
    home_rows = jnp.swapaxes(home, 0, 1).reshape(flight * CAP, model_width)
    total = (home_rows + router_part).astype(jnp.bfloat16)
    token_grads = contract(placing, total, 0, 0).astype(jnp.bfloat16)
    return (token_grads, w_in_grad, w_out_grad, router_grad)


def solution(mesh):
    in_specs = (
        P(("node", "local"), None),
        P(("node", "local"), None),
        P(("node", "local"), None),
        P(("node", "local"), None),
        P(("node", "local"), None),
        P(None, "local", "node"),
        P(None, "node", "local"),
        P(),
    )
    out_specs = (
        P(("node", "local"), None),
        P(None, "local", "node"),
        P(None, "node", "local"),
        P(("node", "local"), None),
    )
    return jax.shard_map(local, mesh=mesh, in_specs=in_specs, out_specs=out_specs, check_vma=False)
```

time: 417 us -> 144 us (0.35)
  the two profiles are of different devices: /device:TPU:0 before, /device:TPU:7 now
where the time goes in v1:
time: 144 us; the launch traced here: 143 us
  Pallas kernels  114 us (79%)
  local copies, waits for them, and re-layouts  10.7 us (7%)
  starting transfers between devices  6.75 us (5%)
  matrix products  5.99 us (4%)
  other arithmetic  4.94 us (3%)
    pallas_call x1, Pallas kernels, run_exchange(): pl.pallas_call(kernel, out_shape=(jax.ShapeDtypeStruct((flight, nodes, 2...  98.8 us
    pallas_call x1, Pallas kernels, weight_grads(): pl.pallas_call(kernel, grid=(flight, steps), in_specs=[pl.BlockSpec((1, n...  15.4 us
    ppermute x1, starting transfers between devices, local(): router_grad = lax.ppermute(part, ('node', 'local'), pairs)  6.75 us
    unnamed x17, local copies, waits for them, and re-layouts  4.72 us
    dot_general x2, matrix products, contract(): lax.dot_general(left, right, (((left_dim,), (right_dim,)), ((), ())), pre...  3.52 us
  transfers between devices with their start and end apart: 1, of which 0 were waited for; matrix products, arithmetic and copies ran while one was open for 4% of the time, Pallas kernels for 11%

profile of v1, /device:TPU:7, one launch (start us, length us, event | category | flops | bytes accessed | tf_op | source)
XLA Modules:
  0.0 143.4 jit_solution(11367746814038249620)
XLA Ops:
  0.7 0.8 compare_select_fusion
  1.5 0.8 subtract_convert_fusion
  2.4 0.4 convolution_convert_fusion.1
  3.0 2.0 %convolution_convert_fusion.2 = bf16[8,8192]{1,0:T(8,128)(2,1)S(1)} fusion(pred[8,128]{1,0:T(8,128)(4,1)S(1)} %fusion.8, bf16[128,8192]{1,0:T(8,128)(2,1)} %param.8), kind=kOutput, calls=%fused_computation.4 | convolution fusion | flops 16842752 | bytes 2229248 | tf_op jit(solution)/shard_map/dot_general | solution.py:424
  5.1 0.2 pad_maximum_fusion
  5.6 0.7 maximum_bitcast_fusion.refs_0_
  6.3 98.8 %exchange.1 = (bf16[2,8,32,2176]{3,2,1,0:T(8,128)(2,1)}, bf16[2,2,128,2048]{3,2,1,0:T(8,128)(2,1)}, f32[16,128]{1,0:T(8,128)}, f32[4,8,2048]{2,1,0:T(8,128)}) custom-call(bf16[4,16,2176]{2,1,0:T(8,128)(2,1)} %maximum_bitcast_fusion.refs_0_, bf16[2,2048,2048]{2,1,0:T(8,128)(2,1)} %refs_1_.1, bf16[2,2048,2048]{2,1,0:T(8,128)(2,1)} %refs_2_.1), custom_call_target="tpu_custom_call" | custom-call | flops 6442450944 | bytes 33554432 | tf_op jit(solution)/shard_map/exchange/pallas_call | solution.py:302
  105.1 0.9 slice.21
  105.9 1.3 slice.27
  107.3 0.7 slice.32
  108.2 0.2 slice_reduce_fusion.1
  108.4 0.7 multiply_convert_fusion
  109.3 0.8 fusion.2
  110.1 6.7 %collective-permute-start = (f32[256,64]{0,1:T(8,128)}, f32[256,64]{0,1:T(8,128)}, u32[]{:S(2)}, u32[]{:S(2)}) collective-permute-start(f32[256,64]{0,1:T(8,128)} %fusion.2), channel_id=1, source_target_pairs={{0,0},{1,8},{2,16},{3,24},{4,1},{5,9},{6,17},{7,25},{8,2},{9,10},{... | collective-permute-start | bytes 196616 | tf_op jit(solution)/shard_map/ppermute | solution.py:454
  116.9 0.7 stack.14
  117.6 0.7 mul.47
  118.4 1.6 %copy-done.2 = bf16[2,8,32,2176]{3,2,1,0:T(8,128)(2,1)S(1)} copy-done((bf16[2,8,32,2176]{3,2,1,0:T(8,128)(2,1)S(1)}, bf16[2,8,32,2176]{3,2,1,0:T(8,128)(2,1)}, u32[]{:S(2)}) %copy-start.2) | copy-done | bytes 2228248
  120.0 1.6 %copy-done.3 = bf16[2,2,128,2048]{3,2,1,0:T(8,128)(2,1)S(1)} copy-done((bf16[2,2,128,2048]{3,2,1,0:T(8,128)(2,1)S(1)}, bf16[2,2,128,2048]{3,2,1,0:T(8,128)(2,1)}, u32[]{:S(2)}) %copy-start.3) | copy-done | bytes 2097176
  121.6 15.4 %weight_grads.1 = (bf16[2,2048,2048]{2,1,0:T(8,128)(2,1)}, bf16[2,2048,2048]{2,1,0:T(8,128)(2,1)}) custom-call(bf16[2,8,32,2176]{3,2,1,0:T(8,128)(2,1)S(1)} %copy-done.2, bf16[2,2,128,2048]{3,2,1,0:T(8,128)(2,1)S(1)} %copy-done.3, bf16[2,2,128,2048]{3,2,1,0:T(8,128)(2,1)S(1)} %copy-done.3, bf16[2,8,32,2176]{3,2,1,0:T(8,128)(2,1)S(1)} %copy-done.2), custom_call_target="tpu_custom_call" | custom-call | flops 4294967296 | bytes 33554432 | tf_op jit(solution)/shard_map/weight_grads/pallas_call | solution.py:376
  137.0 0.7 pad_maximum_fusion.1
  137.7 0.7 constant_dynamic-slice_fusion
  138.4 0.7 fusion.9
  139.2 2.7 %convolution_convert_fusion = bf16[128,8192]{1,0:T(8,128)(2,1)} fusion(pred[8,128]{1,0:T(8,128)(4,1)} %copy-done.6, f32[8,8192]{1,0:T(8,128)S(1)} %bitcast.42, bf16[8,64]{1,0:T(8,128)(2,1)S(1)} %bitcast.47, bf16[8192,64]{0,1:T(8,128)(2,1)S(1)} %copy-done.4), kind=kOutput, calls=%fused_computation | convolution fusion | flops 26345472 | bytes 3409920 | tf_op jit(solution)/shard_map/dot_general | solution.py:31
  141.9 1.5 %copy.46 = f32[256,64]{0,1:T(8,128)} copy(f32[256,64]{0,1:T(8,128)} %collective-permute-done) | data formatting | bytes 131072
  (31 shorter events, 1.1 us)
Async XLA Ops:
  0.6 1.8 %copy-start = (bf16[128,8192]{1,0:T(8,128)(2,1)S(1)}, bf16[128,8192]{1,0:T(8,128)(2,1)}, u32[]{:S(2)}) copy-start(bf16[128,8192]{1,0:T(8,128)(2,1)} %param.9) | copy-start | bytes 6291460
  0.7 107.8 %copy-start.7 = (f32[2,64]{1,0:T(2,128)}, f32[2,64]{1,0:T(2,128)S(1)}, u32[]{:S(2)}) copy-start(f32[2,64]{1,0:T(2,128)S(1)} %compare_convert_fusion) | copy-start | bytes 1540
  1.5 3.9 %copy-start.6 = (pred[8,128]{1,0:T(8,128)(4,1)}, pred[8,128]{1,0:T(8,128)(4,1)S(1)}, u32[]{:S(2)}) copy-start(pred[8,128]{1,0:T(8,128)(4,1)S(1)} %fusion.8) | copy-start | bytes 3076
  110.1 31.8 %collective-permute-start = (f32[256,64]{0,1:T(8,128)}, f32[256,64]{0,1:T(8,128)}, u32[]{:S(2)}, u32[]{:S(2)}) collective-permute-start(f32[256,64]{0,1:T(8,128)} %fusion.2), channel_id=1, source_target_pairs={{0,0},{1,8},{2,16},{3,24},{4,1},{5,9},{6,17},{7,25},{8,2},{9,10},{... | collective-permute-start | bytes 196616 | tf_op jit(solution)/shard_map/ppermute | solution.py:454
  118.4 1.6 %copy-start.2 = (bf16[2,8,32,2176]{3,2,1,0:T(8,128)(2,1)S(1)}, bf16[2,8,32,2176]{3,2,1,0:T(8,128)(2,1)}, u32[]{:S(2)}) copy-start(bf16[2,8,32,2176]{3,2,1,0:T(8,128)(2,1)} %get-tuple-element.11.rows_ref.left_ref) | copy-start | bytes 6684676
  120.0 1.6 %copy-start.3 = (bf16[2,2,128,2048]{3,2,1,0:T(8,128)(2,1)S(1)}, bf16[2,2,128,2048]{3,2,1,0:T(8,128)(2,1)}, u32[]{:S(2)}) copy-start(bf16[2,2,128,2048]{3,2,1,0:T(8,128)(2,1)} %get-tuple-element.13.act_ref.grad_ref) | copy-start | bytes 6291460
  121.6 17.6 %copy-start.4 = (bf16[8192,64]{0,1:T(8,128)(2,1)S(1)}, bf16[8192,64]{0,1:T(8,128)(2,1)}, u32[]{:S(2)}) copy-start(bf16[8192,64]{0,1:T(8,128)(2,1)} %param.15) | copy-start | bytes 3145732
  121.6 17.6 %copy-start.5 = (f32[4,8,2048]{2,1,0:T(8,128)S(1)}, f32[4,8,2048]{2,1,0:T(8,128)}, u32[]{:S(2)}) copy-start(f32[4,8,2048]{2,1,0:T(8,128)} %get-tuple-element.10) | copy-start | bytes 786436
  121.6 21.8 %copy-start.1 = (bf16[128,8192]{1,0:T(8,128)(2,1)S(1)}, bf16[128,8192]{1,0:T(8,128)(2,1)}, u32[]{:S(2)}) copy-start(bf16[128,8192]{1,0:T(8,128)(2,1)} %param.9) | copy-start | bytes 6291460

commit v2 on v1

--- a/solution.py
+++ b/solution.py
@@ -45,7 +45,7 @@
     return jnp.sum(jnp.where(lane == expert, flat, 0.0), axis=1, keepdims=True)
 
 
-def exchange(dims, send, w_in, w_out, rows_out, hidden_out, scores_out, home_out,
+def exchange(dims, send, w_in, w_out, rows_out, hidden_out, part_out, logits_out, home_out,
              w_in_v, w_out_v, first, rows_v, part_s, part_r, own, hidden_v, terms, terms_r,
              core_sum, node_r, grads, home_s, home_r, score_1, score_2, score_3,
              w_sem, out_sem, a_s, a_r, z_s, z_r, c_s, c_r, p_s, p_r, g_s, g_r, t_s, t_r,
@@ -119,29 +119,32 @@
     for e in range(flight):
         rows_v[e, node] = ordered[e * 2 * span:(e + 1) * 2 * span]
 
-    def to_chips(e):
+    def unit(u, at):
+        return rows_v.at[u // 2, at, pl.ds((u % 2) * span, span)]
+
+    def to_chips(u):
         copies = launch([
-            remote(rows_v.at[e, node], rows_v.at[e, node], z_s.at[e, d], z_r.at[e, d], chip_peer(d))
+            remote(unit(u, node), unit(u, node), z_s.at[u, d], z_r.at[u, d], chip_peer(d))
             for d in range(1, chips)
         ])
         return copies, launch([
-            remote(rows_v.at[e, node], rows_v.at[e, node], c_s.at[e, 0], c_r.at[e, 0], sibling)
+            remote(unit(u, node), unit(u, node), c_s.at[u, 0], c_r.at[u, 0], sibling)
         ])
 
-    def finish_rows(e, copies, over):
+    def finish_rows(u, moving):
+        copies, over = moving
         for d in range(1, chips):
             copies[d - 1].wait_recv()
             at = lax.rem(chip + chips - d, chips) * 2 + core
             over = over + launch([
-                remote(rows_v.at[e, at], rows_v.at[e, at], c_s.at[e, d], c_r.at[e, d], sibling)
+                remote(unit(u, at), unit(u, at), c_s.at[u, d], c_r.at[u, d], sibling)
             ])
         return over
 
-    def project(e):
-        loads[2 * e].wait()
-        loads[2 * e + 1].wait()
-        left = rows_v[e, :, 0:span, 0:width].reshape(rows, width)
-        up = rows_v[e, :, span:2 * span, 0:width].reshape(rows, width)
+    def project(u):
+        e, kind = u // 2, u % 2
+        loads[u].wait()
+        left = rows_v[e, :, kind * span:(kind + 1) * span, 0:width].reshape(rows, width)
         copies = []
         tile = min(piece, 256)
         for d in list(range(1, locals_)) + [0]:
@@ -150,45 +153,51 @@
             def column(j, carry):
                 at = pl.ds(pl.multiple_of(base + j * tile, tile), tile)
                 to = pl.ds(pl.multiple_of(j * tile, tile), tile)
-                pre = contract(left, w_in_v[e, :, at], 1, 0)
-                upw = contract(up, w_out_v[e, at, :], 1, 1)
+                if kind == 0:
+                    made = contract(left, w_in_v[e, :, at], 1, 0)
+                else:
+                    made = contract(left, w_out_v[e, at, :], 1, 1)
                 if d == 0:
-                    own[0, :, to] = pre
-                    own[1, :, to] = upw
+                    own[e, kind, :, to] = made
                 else:
-                    part_s[e, d - 1, 0, :, to] = pre.astype(jnp.bfloat16)
-                    part_s[e, d - 1, 1, :, to] = upw.astype(jnp.bfloat16)
+                    part_s[e, d - 1, kind, :, to] = made.astype(jnp.bfloat16)
                 return carry
 
             lax.fori_loop(0, piece // tile, column, 0)
             if d > 0:
                 copies += launch([
-                    remote(part_s.at[e, d - 1], part_r.at[e, d - 1], p_s.at[e, d], p_r.at[e, d],
-                           local_peer(d))
+                    remote(part_s.at[e, d - 1, kind], part_r.at[e, d - 1, kind], p_s.at[u, d],
+                           p_r.at[u, d], local_peer(d))
                 ])
         return copies
+
+    here = pl.ds(pl.multiple_of(loc * piece, piece), piece)
+
+    def spread_hidden(e, kind):
+        mine = hidden_v.at[e, kind, :, here]
+        return launch([
+            remote(mine, mine, g_s.at[2 * e + kind, d], g_r.at[2 * e + kind, d], local_peer(d))
+            for d in range(1, locals_)
+        ])
 
     def hidden_step(e, copies):
         arrive(copies)
         gate = gate_column(rows_v[e, :, 0:span, width:width + PAD], e)
-        pre, upw = own[0], own[1]
+        pre, upw = own[e, 0], own[e, 1]
         for d in range(locals_ - 1):
             pre = pre + part_r[e, d, 0].astype(jnp.float32)
             upw = upw + part_r[e, d, 1].astype(jnp.float32)
         value, slope = gelu_pair(pre)
         act = value.astype(jnp.bfloat16)
-        here = pl.ds(pl.multiple_of(loc * piece, piece), piece)
         hidden_v[e, 0, :, here] = act
         hidden_v[e, 1, :, here] = (gate * upw * slope).astype(jnp.bfloat16)
+        copies = spread_hidden(e, 1)
         score_1[loc, 8 * e:8 * e + 8] = lax.dot_general(
             jnp.ones((8, piece), jnp.float32), act.astype(jnp.float32) * upw,
             (((1,), (1,)), ((), ())), precision=lax.Precision.HIGHEST,
             preferred_element_type=jnp.float32,
         )
-        mine = hidden_v.at[e, :, :, here]
-        return launch([
-            remote(mine, mine, g_s.at[e, d], g_r.at[e, d], local_peer(d)) for d in range(1, locals_)
-        ])
+        return copies
 
     def row_terms(e, copies):
         arrive(copies)
@@ -223,17 +232,55 @@
             total = total + node_r[e, d].astype(jnp.float32)
         grads[e] = total.astype(jnp.bfloat16)
 
-    z_0, over_0 = to_chips(0)
-    over_0 = finish_rows(0, z_0, over_0)
-    z_1, over_1 = to_chips(1)
-    arrive(over_0)
+    def logits(total):
+        made = jnp.zeros(part_out.shape, jnp.float32)
+        me = node * locals_ + loc
+        mine = one_hot_rows(8, rows, lambda i: me * CAP + i)
+        fold = one_hot_rows(PAD, PAD, lambda i: lax.rem(i, PAD // 2))
+        span_out = part_out.shape[0]
+        for e in range(flight):
+            flat = rows_v[e, :, 0:span, width:width + PAD].reshape(rows, PAD)
+            probs = contract(flat, fold, 1, 0)
+            lane = lax.broadcasted_iota(jnp.int32, (rows, PAD), 1)
+            own_prob = jnp.sum(jnp.where(lane == e, probs, 0.0), axis=1, keepdims=True)
+            line = lax.broadcasted_iota(jnp.int32, (8 * flight, PAD), 0)
+            score = lax.dot_general(
+                total, (line == 8 * e).astype(jnp.float32), (((0,), (0,)), ((), ())),
+                precision=lax.Precision.HIGHEST, preferred_element_type=jnp.float32,
+            )
+            hot = (lane == e).astype(jnp.float32)
+            logit = (probs * ((hot - own_prob) * score)).astype(jnp.bfloat16)
+            logits_out[8 * e:8 * e + 8] = contract(mine, logit, 1, 0)
+            if span_out % 128 == 0:
+                at = pl.ds(pl.multiple_of(node * span_out, span_out), span_out)
+                picked = rows_v[e, :, 0:span, at].reshape(rows, span_out)
+            else:
+                left = rows_v[e, :, 0:span, 0:width].reshape(rows, width)
+                line = lax.broadcasted_iota(jnp.int32, (width, span_out), 0)
+                lane = lax.broadcasted_iota(jnp.int32, (width, span_out), 1)
+                chosen = (line == lane + node * span_out).astype(jnp.bfloat16)
+                picked = contract(left, chosen, 1, 0).astype(jnp.bfloat16)
+            made = made + contract(picked, logit, 0, 0)
+        part_out[...] = made
+
+    over = finish_rows(0, to_chips(0))
+    moving = to_chips(1)
+    arrive(over)
     parts_0 = project(0)
-    over_1 = finish_rows(1, z_1, over_1)
+    over = finish_rows(1, moving)
+    moving = to_chips(2)
+    arrive(over)
+    parts_0 += project(1)
+    over = finish_rows(2, moving)
+    moving = to_chips(3)
+    arrive(over)
+    parts_1 = project(2)
     hidden_0 = hidden_step(0, parts_0)
-    arrive(over_1)
+    over = finish_rows(3, moving)
+    arrive(over)
     rows_copy = pltpu.make_async_copy(rows_v, rows_out, out_sem.at[0])
     rows_copy.start()
-    parts_1 = project(1)
+    parts_1 += project(3)
     terms_0 = row_terms(0, hidden_0)
     hidden_1 = hidden_step(1, parts_1)
 
@@ -248,9 +295,11 @@
         remote(score_2.at[chip], score_2.at[chip], s2_s.at[d], s2_r.at[d], chip_peer(d))
         for d in range(1, chips)
     ])
-    terms_1 = row_terms(1, hidden_1)
-    hidden_copy = pltpu.make_async_copy(hidden_v, hidden_out, out_sem.at[1])
-    hidden_copy.start()
+    arrive(hidden_1)
+    acts = spread_hidden(0, 0) + spread_hidden(1, 0)
+    terms_1 = row_terms(1, [])
+    grad_copy = pltpu.make_async_copy(hidden_v.at[:, 1], hidden_out.at[1], out_sem.at[1])
+    grad_copy.start()
     arrive(along)
     score_3[core] = jnp.sum(score_2[...], axis=0)
     across = launch([
@@ -259,7 +308,7 @@
     nodes_1 = reduce_nodes(1, terms_1)
     finish_grads(0, nodes_0)
     arrive(across)
-    scores_out[...] = score_3[0] + score_3[1]
+    logits(score_3[0] + score_3[1])
     finish_grads(1, nodes_1)
 
     def home_source(i):
@@ -275,12 +324,16 @@
         for d in range(1, locals_)
     ])
     home_r[loc] = home_s[loc]
+    arrive(acts)
+    act_copy = pltpu.make_async_copy(hidden_v.at[:, 0], hidden_out.at[0], out_sem.at[2])
+    act_copy.start()
     arrive(home)
     home_out[...] = home_r[...]
     for copy in sent:
         copy.wait_send()
     rows_copy.wait()
-    hidden_copy.wait()
+    grad_copy.wait()
+    act_copy.wait()
 
 
 def run_exchange(send, w_in, w_out, nodes, locals_):
@@ -303,12 +356,13 @@
         kernel,
         out_shape=(
             jax.ShapeDtypeStruct((flight, nodes, 2 * span, wide), half),
-            jax.ShapeDtypeStruct((flight, 2, rows, hidden), half),
-            jax.ShapeDtypeStruct((flight * 8, rows), full),
+            jax.ShapeDtypeStruct((2, flight, rows, hidden), half),
+            jax.ShapeDtypeStruct((width // nodes, PAD), full),
+            jax.ShapeDtypeStruct((flight * 8, PAD), full),
             jax.ShapeDtypeStruct((locals_, flight * CAP, width), full),
         ),
         in_specs=[vmem, hbm, hbm],
-        out_specs=(hbm, hbm, vmem, vmem),
+        out_specs=(hbm, hbm, vmem, vmem, vmem),
         scratch_shapes=[
             pltpu.VMEM((flight, width, hidden), half),
             pltpu.VMEM((flight, hidden, width), half),
@@ -316,7 +370,7 @@
             pltpu.VMEM((flight, nodes, 2 * span, wide), half),
             pltpu.VMEM((flight, locals_ - 1, 2, rows, piece), half),
             pltpu.VMEM((flight, locals_ - 1, 2, rows, piece), half),
-            pltpu.VMEM((2, rows, piece), full),
+            pltpu.VMEM((flight, 2, rows, piece), full),
             pltpu.VMEM((flight, 2, rows, hidden), half),
             pltpu.VMEM((flight, chips, 2, span, width), half),
             pltpu.VMEM((flight, chips, span, width), half),
@@ -328,12 +382,12 @@
             pltpu.VMEM((locals_, flight * 8, rows), full),
             pltpu.VMEM((chips, flight * 8, rows), full),
             pltpu.VMEM((2, flight * 8, rows), full),
-            dma((2 * flight,)), dma((2,)),
+            dma((2 * flight,)), dma((3,)),
             dma((locals_,)), dma((locals_,)),
-            dma((flight, chips)), dma((flight, chips)),
-            dma((flight, chips)), dma((flight, chips)),
-            dma((flight, locals_)), dma((flight, locals_)),
-            dma((flight, locals_)), dma((flight, locals_)),
+            dma((2 * flight, chips)), dma((2 * flight, chips)),
+            dma((2 * flight, chips)), dma((2 * flight, chips)),
+            dma((2 * flight, locals_)), dma((2 * flight, locals_)),
+            dma((2 * flight, locals_)), dma((2 * flight, locals_)),
             dma((flight,)), dma((flight,)),
             dma((flight, chips)), dma((flight, chips)),
             dma((locals_,)), dma((locals_,)),
@@ -357,7 +411,7 @@
     flight, nodes, double, wide = rows_all.shape
     span = double // 2
     rows, hidden = hidden_all.shape[2:]
-    steps = 8
+    steps = 4
     high, low = hidden // steps, width // steps
 
     def kernel(rows_ref, act_ref, grad_ref, left_ref, out_ref, in_ref, out_grad):
@@ -378,8 +432,8 @@
         grid=(flight, steps),
         in_specs=[
             pl.BlockSpec((1, nodes, double, wide), lambda e, s: (e, 0, 0, 0)),
-            pl.BlockSpec((1, 1, rows, high), lambda e, s: (e, 0, 0, s)),
-            pl.BlockSpec((1, 1, rows, hidden), lambda e, s: (e, 1, 0, 0)),
+            pl.BlockSpec((1, 1, rows, high), lambda e, s: (0, e, 0, s)),
+            pl.BlockSpec((1, 1, rows, hidden), lambda e, s: (1, e, 0, 0)),
             pl.BlockSpec((1, nodes, double, low), lambda e, s: (e, 0, 0, s)),
         ],
         out_specs=(
@@ -407,9 +461,6 @@
     experts = router_probs.shape[1]
     nodes = lax.axis_size("node")
     locals_ = lax.axis_size("local")
-    node = lax.axis_index("node")
-    span = locals_ * CAP
-    rows = nodes * span
     is_kept = slot_index >= 0
     target = jnp.where(is_kept, expert_ids * CAP + slot_index, -1)
     slot_iota = jnp.arange(flight * CAP, dtype=jnp.int32)
@@ -432,31 +483,14 @@
     ).reshape(flight * 2 * CAP, locals_, PAD)
     send = jnp.swapaxes(jnp.concatenate([feats, tail], axis=2), 0, 1)
 
-    rows_all, hidden_all, scores, home = run_exchange(send, w_in, w_out, nodes, locals_)
-    w_out_grad, w_in_grad = weight_grads(rows_all, hidden_all, width)
-
-    both = rows_all[:, :, 0:span, width:].reshape(flight, rows, 2, PAD // 2)[:, :, :, :experts]
-    probs_rows = both[:, :, 0].astype(jnp.float32) + both[:, :, 1].astype(jnp.float32)
-    own_prob = jnp.stack([probs_rows[e, :, e] for e in range(flight)])
-    score = scores.reshape(flight, 8, rows)[:, 0, :, None]
-    hot = (jnp.arange(experts)[None, :] == jnp.arange(flight)[:, None]).astype(jnp.float32)
-    logit_rows = probs_rows * ((hot[:, None, :] - own_prob[:, :, None]) * score)
-    logit_rows = logit_rows.astype(jnp.bfloat16)
-
-    block = width // nodes
-    picked = lax.dynamic_slice_in_dim(rows_all[:, :, 0:span], node * block, block, 3)
-    part = contract(
-        picked.reshape(flight * rows, block), logit_rows.reshape(flight * rows, experts), 0, 0
-    )
+    rows_all, hidden_all, part, logits, home = run_exchange(send, w_in, w_out, nodes, locals_)
+
     pairs = [
         (n * locals_ + l, nodes * l + n) for n in range(nodes) for l in range(locals_)
     ]
-    router_grad = lax.ppermute(part, ("node", "local"), pairs)
-
-    me = node * locals_ + lax.axis_index("local")
-    home_logits = lax.dynamic_slice_in_dim(
-        logit_rows.reshape(flight, nodes * locals_, CAP, experts), me, 1, 1
-    )
+    router_grad = lax.ppermute(part[:, :experts], ("node", "local"), pairs)
+    w_out_grad, w_in_grad = weight_grads(rows_all, hidden_all, width)
+    home_logits = logits.reshape(flight, 8, PAD)[:, :CAP, :experts].astype(jnp.bfloat16)
     router_part = contract(home_logits.reshape(flight * CAP, experts), router_weight, 1, 1)
     home_rows = jnp.swapaxes(home, 0, 1).reshape(flight * CAP, model_width)
     total = (home_rows + router_part).astype(jnp.bfloat16)

time: 144 us -> 109 us (0.76)
  Pallas kernels: 114 us -> 89.4 us
  local copies, waits for them, and re-layouts: 10.7 us -> 4.43 us
  other arithmetic: 4.94 us -> 3.32 us
    pallas_call x1, Pallas kernels: 98.8 us -> 76.7 us  [run_exchange(): pl.pallas_call(kernel, out_shape=(jax.ShapeDtypeStruct((flight, nodes, 2...]
    slice x4 -> x1, local copies, waits for them, and re-layouts: 3.06 us -> 0.01 us  [local(): logits.reshape(flight, 8, PAD)[:, :CAP, :experts].astype(jnp.bfloat16)]
    pallas_call x1, Pallas kernels: 15.4 us -> 12.7 us  [weight_grads(): pl.pallas_call(kernel, grid=(flight, steps), in_specs=[pl.BlockSpec((1, n...]
    convert_element_type x3 -> x0, other arithmetic: 1.45 us -> none  [the longest x2 1.45 us: local(): logit_rows = logit_rows.astype(jnp.bfloat16)]
    dot_general x2 -> x1, matrix products: 3.52 us -> 2.13 us  [contract(): lax.dot_general(left, right, (((left_dim,), (right_dim,)), ((), ())), pre...]
    unnamed x17 -> x13, local copies, waits for them, and re-layouts: 4.72 us -> 3.95 us
  transfers between devices with their start and end apart: 1 -> 1, of which waited for: 0 -> 0; matrix products, arithmetic and copies ran while one was open for 4% -> 3% of each run, Pallas kernels for 11% -> 12%
where the time goes in v2:
time: 109 us
  Pallas kernels  89.4 us (82%)
  starting transfers between devices  6.33 us (6%)
  matrix products  4.6 us (4%)
  local copies, waits for them, and re-layouts  4.43 us (4%)
  other arithmetic  3.32 us (3%)
    pallas_call x1, Pallas kernels, run_exchange(): pl.pallas_call(kernel, out_shape=(jax.ShapeDtypeStruct((flight, nodes, 2...  76.7 us
    pallas_call x1, Pallas kernels, weight_grads(): pl.pallas_call(kernel, grid=(flight, steps), in_specs=[pl.BlockSpec((1, n...  12.7 us
    ppermute x1, starting transfers between devices, local(): router_grad = lax.ppermute(part[:, :experts], ('node', 'local'), pairs)  6.33 us
    unnamed x13, local copies, waits for them, and re-layouts  3.95 us
    dot_general x3, matrix products, place(): jnp.dot(placing, array, preferred_element_type=jnp.float32)  2.47 us
  transfers between devices with their start and end apart: 1, of which 0 were waited for; matrix products, arithmetic and copies ran while one was open for 3% of the time, Pallas kernels for 12%

profile of v2, /device:TPU:7, one launch (start us, length us, event | category | flops | bytes accessed | tf_op | source)
XLA Modules:
  0.0 108.8 jit_solution(4314439365964808384)
XLA Ops:
  0.6 0.0 copy-start
  0.6 0.8 compare_select_fusion
  1.5 0.8 subtract_convert_fusion
  2.3 0.0 copy-done
  2.4 0.4 convolution_convert_fusion.1
  2.7 0.1 stack_reshape.7
  2.8 0.1 copy.17
  2.9 2.0 %convolution_convert_fusion.2 = bf16[8,8192]{1,0:T(8,128)(2,1)S(1)} fusion(pred[8,128]{1,0:T(8,128)(4,1)S(1)} %fusion.4, bf16[128,8192]{1,0:T(8,128)(2,1)} %param.8), kind=kOutput, calls=%fused_computation.4 | convolution fusion | flops 16842752 | bytes 2229248 | tf_op jit(solution)/shard_map/dot_general | solution.py:475
  4.9 0.1 stack_reshape.6
  5.0 0.1 copy.16
  5.1 0.2 pad_maximum_fusion
  5.3 0.1 reshape.26
  5.4 0.1 convolution_convert_fusion.3
  5.5 0.7 maximum_bitcast_fusion.refs_0_
  6.3 76.7 %exchange.1 = (bf16[2,8,32,2176]{3,2,1,0:T(8,128)(2,1)}, bf16[2,2,128,2048]{3,2,1,0:T(8,128)(2,1)}, f32[256,128]{1,0:T(8,128)}, f32[16,128]{1,0:T(8,128)}, f32[4,8,2048]{2,1,0:T(8,128)}) custom-call(bf16[4,16,2176]{2,1,0:T(8,128)(2,1)} %maximum_bitcast_fusion.refs_0_, bf16[2,2048,2048]{2,1,0:T(8,128)(2,1)} %refs_1_.1, bf16[2,2048,2048]{2,1,0:T(8,128)(2,1)} %refs_2_.1), custom_call_target="tpu_custom_call" | custom-call | flops 6442450944 | bytes 33554432 | tf_op jit(solution)/shard_map/exchange/pallas_call | solution.py:355
  83.0 6.3 %collective-permute-start = (f32[256,64]{1,0:T(8,128)}, f32[256,64]{1,0:T(8,128)S(1)}, u32[]{:S(2)}, u32[]{:S(2)}) collective-permute-start(f32[256,64]{1,0:T(8,128)} %bitcast.25), channel_id=1, source_target_pairs={{0,0},{1,8},{2,16},{3,24},{4,1},{5,9},{6,17},{7,25},{8,2},{9,10},{... | collective-permute-start | bytes 196616 | tf_op jit(solution)/shard_map/ppermute | solution.py:491
  89.3 0.7 convert_bitcast_fusion
  90.0 1.6 %copy-done.2 = bf16[2,8,32,2176]{3,2,1,0:T(8,128)(2,1)S(1)} copy-done((bf16[2,8,32,2176]{3,2,1,0:T(8,128)(2,1)S(1)}, bf16[2,8,32,2176]{3,2,1,0:T(8,128)(2,1)}, u32[]{:S(2)}) %copy-start.2) | copy-done | bytes 2228248
  91.6 1.6 %copy-done.3 = bf16[2,2,128,2048]{3,2,1,0:T(8,128)(2,1)S(1)} copy-done((bf16[2,2,128,2048]{3,2,1,0:T(8,128)(2,1)S(1)}, bf16[2,2,128,2048]{3,2,1,0:T(8,128)(2,1)}, u32[]{:S(2)}) %copy-start.3) | copy-done | bytes 2097176
  93.2 12.7 %weight_grads.1 = (bf16[2,2048,2048]{2,1,0:T(8,128)(2,1)}, bf16[2,2048,2048]{2,1,0:T(8,128)(2,1)}) custom-call(bf16[2,8,32,2176]{3,2,1,0:T(8,128)(2,1)S(1)} %copy-done.2, bf16[2,2,128,2048]{3,2,1,0:T(8,128)(2,1)S(1)} %copy-done.3, bf16[2,2,128,2048]{3,2,1,0:T(8,128)(2,1)S(1)} %copy-done.3, bf16[2,8,32,2176]{3,2,1,0:T(8,128)(2,1)S(1)} %copy-done.2), custom_call_target="tpu_custom_call" | custom-call | flops 4294967296 | bytes 33554432 | tf_op jit(solution)/shard_map/weight_grads/pallas_call | solution.py:430
  105.9 2.1 %convolution_convert_fusion = bf16[128,8192]{1,0:T(8,128)(2,1)} fusion(pred[8,128]{1,0:T(8,128)(4,1)S(1)} %fusion.4, f32[8,8192]{1,0:T(8,128)S(1)} %bitcast.21, bf16[8,64]{1,0:T(8,128)(2,1)S(1)} %bitcast.23, bf16[8192,64]{0,1:T(8,128)(2,1)S(1)} %copy-done.4), kind=kOutput, calls=%fused_computation | convolution fusion | flops 26345472 | bytes 3409920 | tf_op jit(solution)/shard_map/dot_general | solution.py:31
  108.1 0.0 collective-permute-done
  108.1 0.7 copy.18
  108.8 0.0 copy-done.1
  (11 shorter events, 0.0 us)
Async XLA Ops:
  0.6 1.7 %copy-start = (bf16[128,8192]{1,0:T(8,128)(2,1)S(1)}, bf16[128,8192]{1,0:T(8,128)(2,1)}, u32[]{:S(2)}) copy-start(bf16[128,8192]{1,0:T(8,128)(2,1)} %param.9) | copy-start | bytes 6291460
  83.0 25.1 %collective-permute-start = (f32[256,64]{1,0:T(8,128)}, f32[256,64]{1,0:T(8,128)S(1)}, u32[]{:S(2)}, u32[]{:S(2)}) collective-permute-start(f32[256,64]{1,0:T(8,128)} %bitcast.25), channel_id=1, source_target_pairs={{0,0},{1,8},{2,16},{3,24},{4,1},{5,9},{6,17},{7,25},{8,2},{9,10},{... | collective-permute-start | bytes 196616 | tf_op jit(solution)/shard_map/ppermute | solution.py:491
  90.0 1.6 %copy-start.2 = (bf16[2,8,32,2176]{3,2,1,0:T(8,128)(2,1)S(1)}, bf16[2,8,32,2176]{3,2,1,0:T(8,128)(2,1)}, u32[]{:S(2)}) copy-start(bf16[2,8,32,2176]{3,2,1,0:T(8,128)(2,1)} %get-tuple-element.13.rows_ref.left_ref) | copy-start | bytes 6684676
  91.6 1.6 %copy-start.3 = (bf16[2,2,128,2048]{3,2,1,0:T(8,128)(2,1)S(1)}, bf16[2,2,128,2048]{3,2,1,0:T(8,128)(2,1)}, u32[]{:S(2)}) copy-start(bf16[2,2,128,2048]{3,2,1,0:T(8,128)(2,1)} %get-tuple-element.14.act_ref.grad_ref) | copy-start | bytes 6291460
  93.2 12.7 %copy-start.4 = (bf16[8192,64]{0,1:T(8,128)(2,1)S(1)}, bf16[8192,64]{0,1:T(8,128)(2,1)}, u32[]{:S(2)}) copy-start(bf16[8192,64]{0,1:T(8,128)(2,1)} %param.15) | copy-start | bytes 3145732
  93.2 12.7 %copy-start.5 = (f32[4,8,2048]{2,1,0:T(8,128)S(1)}, f32[4,8,2048]{2,1,0:T(8,128)}, u32[]{:S(2)}) copy-start(f32[4,8,2048]{2,1,0:T(8,128)} %get-tuple-element.11) | copy-start | bytes 786436
  93.2 15.6 %copy-start.1 = (bf16[128,8192]{1,0:T(8,128)(2,1)S(1)}, bf16[128,8192]{1,0:T(8,128)(2,1)}, u32[]{:S(2)}) copy-start(bf16[128,8192]{1,0:T(8,128)(2,1)} %param.9) | copy-start | bytes 6291460

commit v3 on v2

--- a/solution.py
+++ b/solution.py
@@ -199,38 +199,61 @@
         )
         return copies
 
-    def row_terms(e, copies):
-        arrive(copies)
-        tile = min(width, 512)
+    half_width = width // 2
+
+    def row_terms(e, h):
+        tile = min(half_width, 512)
 
         def column(j, carry):
-            at = pl.ds(pl.multiple_of(j * tile, tile), tile)
+            at = pl.ds(pl.multiple_of(h * half_width + j * tile, tile), tile)
             made = contract(hidden_v[e, 1], w_in_v[e, at, :], 1, 1).astype(jnp.bfloat16)
             terms[e, :, :, :, at] = made.reshape(chips, 2, span, tile)
             return carry
 
-        lax.fori_loop(0, width // tile, column, 0)
+        lax.fori_loop(0, half_width // tile, column, 0)
+        cut = pl.ds(h * half_width, half_width)
         return launch([
-            remote(terms.at[e, :, 1 - core], terms_r.at[e], t_s.at[e], t_r.at[e], sibling)
+            remote(terms.at[e, :, 1 - core, :, cut], terms_r.at[e, :, :, cut], t_s.at[2 * e + h],
+                   t_r.at[2 * e + h], sibling)
         ])
 
-    def reduce_nodes(e, copies):
+    def reduce_nodes(e, h, copies):
         arrive(copies)
-        core_sum[e] = (
-            terms[e, :, core].astype(jnp.float32) + terms_r[e].astype(jnp.float32)
+        cut = pl.ds(h * half_width, half_width)
+        core_sum[e, :, :, cut] = (
+            terms[e, :, core, :, cut].astype(jnp.float32)
+            + terms_r[e, :, :, cut].astype(jnp.float32)
         ).astype(jnp.bfloat16)
         return launch([
-            remote(core_sum.at[e, lax.rem(chip + d, chips)], node_r.at[e, d - 1], n_s.at[e, d],
-                   n_r.at[e, d], chip_peer(d))
+            remote(core_sum.at[e, lax.rem(chip + d, chips), :, cut], node_r.at[e, d - 1, :, cut],
+                   n_s.at[2 * e + h, d], n_r.at[2 * e + h, d], chip_peer(d))
             for d in range(1, chips)
         ])
 
-    def finish_grads(e, copies):
+    def finish_grads(e, h, copies):
         arrive(copies)
-        total = core_sum[e, chip].astype(jnp.float32)
+        cut = pl.ds(h * half_width, half_width)
+        total = core_sum[e, chip, :, cut].astype(jnp.float32)
         for d in range(chips - 1):
-            total = total + node_r[e, d].astype(jnp.float32)
-        grads[e] = total.astype(jnp.bfloat16)
+            total = total + node_r[e, d, :, cut].astype(jnp.float32)
+        grads[e, :, cut] = total.astype(jnp.bfloat16)
+
+    def home_source(i):
+        at, rest = i // (flight * CAP), lax.rem(i, flight * CAP)
+        return (rest // CAP) * span + at * CAP + lax.rem(rest, CAP)
+
+    def send_home(h):
+        cut = pl.ds(h * half_width, half_width)
+        pick = one_hot_rows(locals_ * flight * CAP, flight * span, home_source)
+        picked = contract(pick, grads[:, :, cut].reshape(flight * span, half_width), 1, 0)
+        home_s[:, :, cut] = picked.reshape(locals_, flight * CAP, half_width)
+        copies = launch([
+            remote(home_s.at[lax.rem(loc + d, locals_), :, cut], home_r.at[loc, :, cut],
+                   h_s.at[h, d], h_r.at[h, d], local_peer(d))
+            for d in range(1, locals_)
+        ])
+        home_r[loc, :, cut] = home_s[loc, :, cut]
+        return copies
 
     def logits(total):
         made = jnp.zeros(part_out.shape, jnp.float32)
@@ -281,14 +304,15 @@
     rows_copy = pltpu.make_async_copy(rows_v, rows_out, out_sem.at[0])
     rows_copy.start()
     parts_1 += project(3)
-    terms_0 = row_terms(0, hidden_0)
+    arrive(hidden_0)
+    terms_0 = [row_terms(0, h) for h in range(2)]
     hidden_1 = hidden_step(1, parts_1)
 
     near = launch([
         remote(score_1.at[loc], score_1.at[loc], s1_s.at[d], s1_r.at[d], local_peer(d))
         for d in range(1, locals_)
     ])
-    nodes_0 = reduce_nodes(0, terms_0)
+    nodes_0 = [reduce_nodes(0, h, terms_0[h]) for h in range(2)]
     arrive(near)
     score_2[chip] = jnp.sum(score_1[...], axis=0)
     along = launch([
@@ -297,7 +321,8 @@
     ])
     arrive(hidden_1)
     acts = spread_hidden(0, 0) + spread_hidden(1, 0)
-    terms_1 = row_terms(1, [])
+    terms_1 = [row_terms(1, h) for h in range(2)]
+    nodes_1 = [reduce_nodes(1, 0, terms_1[0])]
     grad_copy = pltpu.make_async_copy(hidden_v.at[:, 1], hidden_out.at[1], out_sem.at[1])
     grad_copy.start()
     arrive(along)
@@ -305,25 +330,15 @@
     across = launch([
         remote(score_3.at[core], score_3.at[core], s3_s.at[0], s3_r.at[0], sibling)
     ])
-    nodes_1 = reduce_nodes(1, terms_1)
-    finish_grads(0, nodes_0)
+    nodes_1 += [reduce_nodes(1, 1, terms_1[1])]
+    for h in range(2):
+        finish_grads(0, h, nodes_0[h])
     arrive(across)
     logits(score_3[0] + score_3[1])
-    finish_grads(1, nodes_1)
-
-    def home_source(i):
-        at, rest = i // (flight * CAP), lax.rem(i, flight * CAP)
-        return (rest // CAP) * span + at * CAP + lax.rem(rest, CAP)
-
-    pick = one_hot_rows(locals_ * flight * CAP, flight * span, home_source)
-    picked = contract(pick, grads[...].reshape(flight * span, width), 1, 0)
-    home_s[...] = picked.reshape(locals_, flight * CAP, width)
-    home = launch([
-        remote(home_s.at[lax.rem(loc + d, locals_)], home_r.at[loc], h_s.at[d], h_r.at[d],
-               local_peer(d))
-        for d in range(1, locals_)
-    ])
-    home_r[loc] = home_s[loc]
+    home = []
+    for h in range(2):
+        finish_grads(1, h, nodes_1[h])
+        home += send_home(h)
     arrive(acts)
     act_copy = pltpu.make_async_copy(hidden_v.at[:, 0], hidden_out.at[0], out_sem.at[2])
     act_copy.start()
@@ -388,9 +403,9 @@
             dma((2 * flight, chips)), dma((2 * flight, chips)),
             dma((2 * flight, locals_)), dma((2 * flight, locals_)),
             dma((2 * flight, locals_)), dma((2 * flight, locals_)),
-            dma((flight,)), dma((flight,)),
-            dma((flight, chips)), dma((flight, chips)),
-            dma((locals_,)), dma((locals_,)),
+            dma((2 * flight,)), dma((2 * flight,)),
+            dma((2 * flight, chips)), dma((2 * flight, chips)),
+            dma((2, locals_)), dma((2, locals_)),
             dma((locals_,)), dma((locals_,)),
             dma((chips,)), dma((chips,)),
             dma((1,)), dma((1,)),
@@ -445,7 +460,7 @@
             jax.ShapeDtypeStruct((flight, width, hidden), jnp.bfloat16),
         ),
         scratch_shapes=[pltpu.VMEM((rows, width), jnp.bfloat16)],
-        compiler_params=pltpu.CompilerParams(vmem_limit_bytes=40 * 1024 * 1024),
+        compiler_params=pltpu.CompilerParams(vmem_limit_bytes=VMEM_BYTES),
         cost_estimate=pl.CostEstimate(
             flops=4 * flight * rows * width * hidden,
             bytes_accessed=4 * flight * width * hidden,

time: 109 us -> 108 us (level)
  local copies, waits for them, and re-layouts: 4.43 us -> 1.21 us
  Pallas kernels: 89.4 us -> 90.8 us
    unnamed x13 -> x9, local copies, waits for them, and re-layouts: 3.95 us -> 0.74 us
    pallas_call x1, Pallas kernels: 12.7 us -> 15.9 us  [weight_grads(): pl.pallas_call(kernel, grid=(flight, steps), in_specs=[pl.BlockSpec((1, n...]
    pallas_call x1, Pallas kernels: 76.7 us -> 74.9 us  [run_exchange(): pl.pallas_call(kernel, out_shape=(jax.ShapeDtypeStruct((flight, nodes, 2...]
  transfers between devices with their start and end apart: 1 -> 1, of which waited for: 0 -> 0; matrix products, arithmetic and copies ran while one was open for 3% -> 3% of each run, Pallas kernels for 12% -> 15%
where the time goes in v3:
time: 108 us
  Pallas kernels  90.8 us (84%)
  starting transfers between devices  6.93 us (6%)
  matrix products  4.6 us (4%)
  other arithmetic  3.32 us (3%)
  local copies, waits for them, and re-layouts  1.21 us (1%)
    pallas_call x1, Pallas kernels, run_exchange(): pl.pallas_call(kernel, out_shape=(jax.ShapeDtypeStruct((flight, nodes, 2...  74.9 us
    pallas_call x1, Pallas kernels, weight_grads(): pl.pallas_call(kernel, grid=(flight, steps), in_specs=[pl.BlockSpec((1, n...  15.9 us
    ppermute x1, starting transfers between devices, local(): router_grad = lax.ppermute(part[:, :experts], ('node', 'local'), pairs)  6.93 us
    dot_general x3, matrix products, place(): jnp.dot(placing, array, preferred_element_type=jnp.float32)  2.47 us
  transfers between devices with their start and end apart: 1, of which 0 were waited for; matrix products, arithmetic and copies ran while one was open for 3% of the time, Pallas kernels for 15%

profile of v3, /device:TPU:7, one launch (start us, length us, event | category | flops | bytes accessed | tf_op | source)
XLA Modules:
  0.0 107.6 jit_solution(445380972109637203)
XLA Ops:
  0.6 0.0 copy-start
  0.6 0.8 compare_select_fusion
  1.5 0.8 subtract_convert_fusion
  2.3 0.0 copy-done
  2.4 0.4 convolution_convert_fusion.1
  2.7 0.1 stack_reshape.7
  2.8 0.1 copy.17
  2.9 2.0 %convolution_convert_fusion.2 = bf16[8,8192]{1,0:T(8,128)(2,1)S(1)} fusion(pred[8,128]{1,0:T(8,128)(4,1)S(1)} %fusion.4, bf16[128,8192]{1,0:T(8,128)(2,1)} %param.8), kind=kOutput, calls=%fused_computation.4 | convolution fusion | flops 16842752 | bytes 2229248 | tf_op jit(solution)/shard_map/dot_general | solution.py:490
  4.9 0.1 stack_reshape.6
  5.0 0.1 copy.16
  5.1 0.2 pad_maximum_fusion
  5.3 0.1 reshape.26
  5.4 0.1 convolution_convert_fusion.3
  5.5 0.7 maximum_bitcast_fusion.refs_0_
  6.3 74.9 %exchange.1 = (bf16[2,8,32,2176]{3,2,1,0:T(8,128)(2,1)}, bf16[2,2,128,2048]{3,2,1,0:T(8,128)(2,1)}, f32[256,128]{1,0:T(8,128)}, f32[16,128]{1,0:T(8,128)}, f32[4,8,2048]{2,1,0:T(8,128)}) custom-call(bf16[4,16,2176]{2,1,0:T(8,128)(2,1)} %maximum_bitcast_fusion.refs_0_, bf16[2,2048,2048]{2,1,0:T(8,128)(2,1)} %refs_1_.1, bf16[2,2048,2048]{2,1,0:T(8,128)(2,1)} %refs_2_.1), custom_call_target="tpu_custom_call" | custom-call | flops 6442450944 | bytes 33554432 | tf_op jit(solution)/shard_map/exchange/pallas_call | solution.py:370
  81.2 6.9 %collective-permute-start = (f32[256,64]{1,0:T(8,128)}, f32[256,64]{1,0:T(8,128)S(1)}, u32[]{:S(2)}, u32[]{:S(2)}) collective-permute-start(f32[256,64]{1,0:T(8,128)} %bitcast.25), channel_id=1, source_target_pairs={{0,0},{1,8},{2,16},{3,24},{4,1},{5,9},{6,17},{7,25},{8,2},{9,10},{... | collective-permute-start | bytes 196616 | tf_op jit(solution)/shard_map/ppermute | solution.py:506
  88.1 0.7 convert_bitcast_fusion
  88.8 0.0 copy-start.1
  88.8 15.9 %weight_grads.1 = (bf16[2,2048,2048]{2,1,0:T(8,128)(2,1)}, bf16[2,2048,2048]{2,1,0:T(8,128)(2,1)}) custom-call(bf16[2,8,32,2176]{3,2,1,0:T(8,128)(2,1)} %get-tuple-element.13.rows_ref.left_ref, bf16[2,2,128,2048]{3,2,1,0:T(8,128)(2,1)} %get-tuple-element.14.act_ref.grad_ref, bf16[2,2,128,2048]{3,2,1,0:T(8,128)(2,1)} %get-tuple-element.14.act_ref.grad_ref, ...), custom_call_target="tpu_custom_call" | custom-call | flops 4294967296 | bytes 33554432 | tf_op jit(solution)/shard_map/weight_grads/pallas_call | solution.py:445
  104.7 0.0 copy-done.2
  104.7 0.0 copy-done.3
  104.7 2.1 %convolution_convert_fusion = bf16[128,8192]{1,0:T(8,128)(2,1)} fusion(pred[8,128]{1,0:T(8,128)(4,1)S(1)} %fusion.4, f32[8,8192]{1,0:T(8,128)S(1)} %bitcast.21, bf16[8,64]{1,0:T(8,128)(2,1)S(1)} %bitcast.23, bf16[8192,64]{0,1:T(8,128)(2,1)S(1)} %copy-done.2), kind=kOutput, calls=%fused_computation | convolution fusion | flops 26345472 | bytes 3409920 | tf_op jit(solution)/shard_map/dot_general | solution.py:31
  106.8 0.0 collective-permute-done
  106.8 0.7 copy.18
  (7 shorter events, 0.0 us)
Async XLA Ops:
  0.6 1.7 %copy-start = (bf16[128,8192]{1,0:T(8,128)(2,1)S(1)}, bf16[128,8192]{1,0:T(8,128)(2,1)}, u32[]{:S(2)}) copy-start(bf16[128,8192]{1,0:T(8,128)(2,1)} %param.9) | copy-start | bytes 6291460
  81.2 25.7 %collective-permute-start = (f32[256,64]{1,0:T(8,128)}, f32[256,64]{1,0:T(8,128)S(1)}, u32[]{:S(2)}, u32[]{:S(2)}) collective-permute-start(f32[256,64]{1,0:T(8,128)} %bitcast.25), channel_id=1, source_target_pairs={{0,0},{1,8},{2,16},{3,24},{4,1},{5,9},{6,17},{7,25},{8,2},{9,10},{... | collective-permute-start | bytes 196616 | tf_op jit(solution)/shard_map/ppermute | solution.py:506
  88.8 15.9 %copy-start.2 = (bf16[8192,64]{0,1:T(8,128)(2,1)S(1)}, bf16[8192,64]{0,1:T(8,128)(2,1)}, u32[]{:S(2)}) copy-start(bf16[8192,64]{0,1:T(8,128)(2,1)} %param.15) | copy-start | bytes 3145732
  88.8 15.9 %copy-start.3 = (f32[4,8,2048]{2,1,0:T(8,128)S(1)}, f32[4,8,2048]{2,1,0:T(8,128)}, u32[]{:S(2)}) copy-start(f32[4,8,2048]{2,1,0:T(8,128)} %get-tuple-element.11) | copy-start | bytes 786436
  88.8 18.7 %copy-start.1 = (bf16[128,8192]{1,0:T(8,128)(2,1)S(1)}, bf16[128,8192]{1,0:T(8,128)(2,1)}, u32[]{:S(2)}) copy-start(bf16[128,8192]{1,0:T(8,128)(2,1)} %param.9) | copy-start | bytes 6291460
